TPU v7x, 256 devices: a whole 4x4x8 slice. The times are simulated.
256 devices in a mesh: slab: 64 (over x, z, core), col: 4 (over y).
Axes of the slice: x: 4, y: 4, z: 8, core: 2. Of those that a mesh axis runs over, the one named last changes fastest.
Arguments:
- pressure: float32 [4096, 1024], P('slab', 'col'), may hold values from 1 to 4
- storage: float32 [4096, 1024], P('slab', 'col'), may hold values from 0.5 to 2
- trans: float32 [4096, 1024], P('slab', 'col'), may hold values from 0.5 to 8
- source: float32 [4096, 1024], P('slab', 'col'), may hold values from -1.2 to 1.2
- shells_old: float32 [4, 4096, 64, 128], P('col', 'slab'), may hold values from 1 to 2
- shell_cap: float32 [64], replicated, may hold values from 0.5 to 4
- shell_trans: float32 [64], replicated, may hold values from 0.5 to 4
- new_source: int32 [4, 2048], P('col'), may hold values from 0 to 4095, as said below
- cell_block: int32 [4, 4096], P('col', 'slab'), may hold values from 0 to 127, as said below
Outputs:
- pressure_out: float32 [4096, 1024], P('slab', 'col')
- shells_new: float32 [4, 2048, 64, 128], P('col', 'slab')
Inputs may be any that keep to these rules, and one draw needn't show every extreme that they name: `new_source`: within each col index, every old slot is taken at most once; the slots after the move on one slab device take blocks from 8 distinct slab devices, exactly 4 blocks from each; the taken old slots lie only on the even-numbered slab devices, each of which has all 64 of its slots taken. `cell_block`: within one slab device and col index the entries are distinct.
All inputs are finite; a program needn't handle non-finite values.
Results may differ from a plain program's by a relative error of at most 0.0003.
Values sent between devices are 32-bit elements; how exact they have to be, the bound alone decides.
A program may use at most 128 MiB of HBM per device.

v0:
```python
import jax
import jax.numpy as jnp
from jax import lax
from jax.sharding import PartitionSpec as P

CAP = 4
STEPS = 2
ITERS = 3
HI = lax.Precision.HIGHEST


def with_halo(shard, sides, width):
    for axis, dim in sides:
        size, length = (lax.axis_size(axis), shard.shape[dim])
        up = [(i, (i + 1) % size) for i in range(size - 1)]
        down = [(j, i) for i, j in up]
        last = lax.slice_in_dim(shard, length - width, length, axis=dim)
        initial = lax.slice_in_dim(shard, 0, width, axis=dim)
        before = lax.ppermute(last, axis, up)
        after = lax.ppermute(initial, axis, down)
        shard = jnp.concatenate([before, shard, after], axis=dim)
    return shard


def shift_rows(x, s):
    z = jnp.zeros((abs(s),) + x.shape[1:], x.dtype)
    return jnp.concatenate([z, x[:-s]], 0) if s > 0 else jnp.concatenate([x[-s:], z], 0)


def shell_inverse(cap, tr):
    n = cap.shape[0]
    inner = jnp.concatenate([tr[1:], jnp.zeros((1,), jnp.float32)])
    b = (cap + tr + inner)[:, None]
    c = -inner[:, None]
    a = jnp.concatenate([jnp.zeros((1, 1), jnp.float32), c[:-1]], 0)
    rhs = jnp.eye(n, dtype=jnp.float32)
    one = jnp.ones_like(b)
    s = 1
    while s < n:
        bm = jnp.concatenate([one[:s], b[:-s]], 0)
        bp = jnp.concatenate([b[s:], one[:s]], 0)
        al, ga = -a / bm, -c / bp
        rhs = rhs + al * shift_rows(rhs, s) + ga * shift_rows(rhs, -s)
        b = b + al * shift_rows(c, s) + ga * shift_rows(a, -s)
        a, c = al * shift_rows(a, s), ga * shift_rows(c, -s)
        s *= 2
    inverse = rhs / b
    return inverse, inverse[:, 0] * tr[0]


def shards(pressure, storage, trans, source, shells_old, shell_cap, shell_trans, new_source, cell_block):
    slab_count = lax.axis_size("slab")
    own = lax.axis_index("slab")
    height, breadth = pressure.shape
    old_slots = shells_old.shape[1]
    nsh = shells_old.shape[2]
    table = new_source[0]
    new_slots = table.shape[0] // slab_count
    inverse, couple = shell_inverse(shell_cap, shell_trans)
    coupling = shell_trans[0] * (1.0 - couple[0])
    amat = inverse * shell_cap[None, :]
    asq = jnp.dot(amat, amat, precision=HI)
    acouple = jnp.dot(amat, couple, precision=HI)
    anchor = (table // old_slots).reshape(slab_count, new_slots)
    local_old = (table % old_slots).reshape(slab_count, new_slots)
    hit = anchor == own
    earlier = jnp.arange(new_slots)[:, None] < jnp.arange(new_slots)[None, :]
    before = jnp.sum(hit[:, :, None] & earlier[None], 1)
    slot = jnp.stack([jnp.sum(jnp.where(hit & (before == r), local_old, 0), 1) for r in range(CAP)], 1)
    own_anchor = lax.dynamic_index_in_dim(anchor, own, 0, keepdims=False)
    idx = jnp.arange(new_slots)
    own_rank = jnp.sum((own_anchor[:, None] == own_anchor[None, :]) & (idx[:, None] > idx[None, :]), 1)
    recv_pos = own_anchor * CAP + own_rank
    state = shells_old[0]
    even = (own % 2 == 0).astype(jnp.float32)
    cb = cell_block[0]
    onehot = (cb[None, :] == jnp.arange(height * breadth // 128)[:, None]).astype(jnp.float32) * even
    rows = jnp.einsum("rk,okc->roc", jnp.stack([amat[0], asq[0]]), state, precision=HI) * shell_trans[0]
    spread = jnp.einsum("fo,roc->rfc", onehot, rows, precision=HI).reshape(2, height, breadth)
    ak = jnp.broadcast_to(jnp.sum(onehot, 1)[:, None] * coupling, (onehot.shape[0], 128)).reshape(height, breadth)
    c2 = shell_trans[0] * jnp.dot(amat[0], couple, precision=HI)
    act = jnp.broadcast_to(jnp.sum(onehot, 1)[:, None], (onehot.shape[0], 128)).reshape(height, breadth)
    tpad = with_halo(trans, (("slab", 0), ("col", 1)), 1)
    shifts = ((0, 1), (2, 1), (1, 0), (1, 2))
    faces = []
    for r, c in shifts:
        near = tpad[r : r + height, c : c + breadth]
        faces.append(2.0 * trans * near / (trans + near))
    conduct = faces[0] + faces[1] + faces[2] + faces[3]
    current = pressure
    saved = []
    for step in range(STEPS):
        prev = current
        base = spread[0] if step == 0 else spread[1] + act * c2 * saved[0]
        for sweep in range(ITERS):
            if sweep == ITERS - 1:
                saved.append(current)
            padded = with_halo(current, (("slab", 0), ("col", 1)), 1)
            flux = jnp.zeros_like(current)
            for (r, c), face in zip(shifts, faces):
                near = padded[r : r + height, c : c + breadth]
                flux = flux + face * 0.5 * (near + current) * (near - current)
            misfit = storage * (current - prev) - flux + (ak * current - base) - source
            current = current - misfit / (storage + current * conduct + ak)
    pb = [jnp.dot(onehot.T, s.reshape(-1, 128), precision=HI) for s in saved]
    final = jnp.einsum("kl,olc->okc", asq, state, precision=HI)
    final = final + acouple[None, :, None] * pb[0][:, None] + couple[None, :, None] * pb[1][:, None]
    pick = (slot.reshape(-1, 1) == jnp.arange(old_slots)[None, :]).astype(jnp.float32)
    outgoing = jnp.dot(pick, final.reshape(old_slots, -1), precision=HI).reshape(slab_count, CAP, nsh, 128)
    arrived = lax.all_to_all(outgoing, "slab", split_axis=0, concat_axis=0, tiled=True)
    take = (recv_pos[:, None] == jnp.arange(slab_count * CAP)[None, :]).astype(jnp.float32)
    out = jnp.dot(take, arrived.reshape(slab_count * CAP, -1), precision=HI).reshape(new_slots, nsh, 128)
    return current, out[None]


def solution(mesh):
    f = P("slab", "col")
    return jax.shard_map(
        shards,
        mesh=mesh,
        in_specs=(f, f, f, f, P("col", "slab", None, None), P(), P(), P("col", None), P("col", "slab")),
        out_specs=(f, P("col", "slab", None, None)),
        check_vma=False,
    )
```

profile of v0, /device:TPU:1, one launch (start us, length us, event | category | flops | bytes accessed | tf_op | source)
XLA Modules:
  0.0 366.3 jit_solution(6159616242664346309)
XLA Ops:
  1.5 5.1 %collective-permute-start.2 = (f32[1,256]{1,0:T(1,128)S(1)}, f32[1,256]{1,0:T(1,128)S(1)}, u32[]{:S(2)}, u32[]{:S(2)}) collective-permute-start(f32[1,256]{1,0:T(1,128)S(1)} %get-tuple-element.72), channel_id=1, source_target_pairs={{4,0},{8,4},{12,8},{16,12},{20,16},{24,20},{28,24},{32,28},{36,32}... | collective-permute-start | bytes 3080 | tf_op jit(solution)/shard_map/ppermute | solution.py:20
  9.3 2.2 collective-permute-start.1
  11.5 2.1 collective-permute-start.3
  28.0 3.0 collective-permute-start.5
  33.7 4.6 %collective-permute-start.4 = (f32[66,1]{1,0:T(8,128)S(1)}, f32[66,1]{1,0:T(8,128)S(1)}, u32[]{:S(2)}, u32[]{:S(2)}) collective-permute-start(f32[66,1]{1,0:T(8,128)S(1)} %get-tuple-element.59), channel_id=1, source_target_pairs={{0,1},{1,2},{2,3},{4,5},{5,6},{6,7},{8,9},{9,10},{10,11},{12,13},{... | collective-permute-start | bytes 800 | tf_op jit(solution)/shard_map/ppermute | solution.py:19
  39.8 5.1 %collective-permute-start.8 = (f32[1,256]{1,0:T(1,128)S(1)}, f32[1,256]{1,0:T(1,128)S(1)}, u32[]{:S(2)}, u32[]{:S(2)}) collective-permute-start(f32[1,256]{1,0:T(1,128)S(1)} %get-tuple-element.70), channel_id=1, source_target_pairs={{0,4},{4,8},{8,12},{12,16},{16,20},{20,24},{24,28},{28,32},{32,36}... | collective-permute-start | bytes 3080 | tf_op jit(solution)/shard_map/ppermute | solution.py:19
  46.8 2.9 collective-permute-done.9
  49.8 3.9 %collective-permute-start.10 = (f32[66,1]{1,0:T(8,128)S(1)}, f32[66,1]{1,0:T(8,128)S(1)}, u32[]{:S(2)}, u32[]{:S(2)}) collective-permute-start(f32[66,1]{1,0:T(8,128)S(1)} %get-tuple-element.56), channel_id=1, source_target_pairs={{0,1},{1,2},{2,3},{4,5},{5,6},{6,7},{8,9},{9,10},{10,11},{12,13},{... | collective-permute-start | bytes 800 | tf_op jit(solution)/shard_map/ppermute | solution.py:19
  55.1 3.7 collective-permute-done.11
  59.0 3.1 collective-permute-start.12
  64.2 2.7 collective-permute-done.13
  67.1 3.6 collective-permute-start.14
  72.1 3.4 collective-permute-done.15
  75.6 3.7 collective-permute-start.16
  79.3 1.9 collective-permute-start.17
  81.4 2.8 collective-permute-done.17
  84.3 3.2 collective-permute-start.18
  89.1 3.1 collective-permute-done.19
  92.5 4.4 %collective-permute-start.20 = (f32[1,256]{1,0:T(1,128)S(1)}, f32[1,256]{1,0:T(1,128)S(1)}, u32[]{:S(2)}, u32[]{:S(2)}) collective-permute-start(f32[1,256]{1,0:T(1,128)S(1)} %get-tuple-element.64), channel_id=1, source_target_pairs={{0,4},{4,8},{8,12},{12,16},{16,20},{20,24},{24,28},{28,32},{32,36}... | collective-permute-start | bytes 3080 | tf_op jit(solution)/shard_map/ppermute | solution.py:19
  99.0 2.9 collective-permute-done.21
  105.3 3.0 collective-permute-done.23
  108.8 2.3 fusion.2
  111.1 4.5 %fusion = f32[64,4,64,128]{3,0,2,1:T(8,128)S(1)} fusion(s32[64,4]{0,1:T(4,128)S(1)} %pad_add_fusion, f32[8,8,64,128]{3,2,1,0:T(8,128)S(1)} %bitcast.211), kind=kOutput, calls=%fused_computation.3 | convolution fusion | flops 1610629120 | bytes 10486784 | tf_op jit(solution)/shard_map/dot_general | solution.py:109
  115.6 8.1 %copy.54 = f32[64,4,64,128]{3,2,1,0:T(8,128)} copy(f32[64,4,64,128]{3,0,2,1:T(8,128)S(1)} %fusion) | data formatting | bytes 16777216 | tf_op jit(solution)/shard_map/dot_general | solution.py:109
  123.7 21.1 %all-to-all-start = ((f32[64,4,64,128]{3,2,1,0:T(8,128)}), f32[64,4,64,128]{3,2,1,0:T(8,128)}, u32[]{:S(2)}, u32[]{:S(2)}) async-start(f32[64,4,64,128]{3,2,1,0:T(8,128)} %copy.54), calls=%async_computation | async-start | bytes 16777216 | tf_op jit(solution)/shard_map/all_to_all | solution.py:110
  145.0 3.5 collective-permute-start.24
  150.7 172.8 %collective-permute-done.24 = f32[1,256]{1,0:T(1,128)S(1)} collective-permute-done((f32[1,256]{1,0:T(1,128)S(1)}, f32[1,256]{1,0:T(1,128)S(1)}, u32[]{:S(2)}, u32[]{:S(2)}) %collective-permute-start.24) | collective-permute-done | bytes 1056 | tf_op jit(solution)/shard_map/ppermute | solution.py:19
  323.4 3.9 %collective-permute-done.25 = f32[1,256]{1,0:T(1,128)S(1)} collective-permute-done((f32[1,256]{1,0:T(1,128)S(1)}, f32[1,256]{1,0:T(1,128)S(1)}, u32[]{:S(2)}, u32[]{:S(2)}) %collective-permute-start.25) | collective-permute-done | bytes 1056 | tf_op jit(solution)/shard_map/ppermute | solution.py:20
  330.6 3.4 collective-permute-done.27
  334.8 14.3 %copy.83 = f32[32,8,64,128]{3,1,2,0:T(8,128)} copy(f32[32,8,64,128]{3,2,1,0:T(8,128)} %bitcast.57) | data formatting | bytes 16777216
  349.1 9.0 %copy.55 = f32[8192,256]{1,0:T(8,128)} copy(f32[8192,256]{0,1:T(8,128)} %bitcast.210) | data formatting | bytes 16777216 | tf_op jit(solution)/shard_map/dot_general | solution.py:112
  358.2 6.6 %convolution_bitcast_fusion = f32[1,32,64,128]{3,1,2,0:T(8,128)S(1)} fusion(f32[64,128,256]{2,1,0:T(8,128)} %bitcast.209, s32[32]{0:T(128)S(1)} %multiply_add_fusion.5), kind=kOutput, calls=%fused_computation.11 | convolution fusion | flops 805314560 | bytes 9437312 | tf_op jit(solution)/shard_map/dot_general | solution.py:112
  (158 shorter events, 42.2 us)
Async XLA Ops:
  0.6 23.6 %copy-start = (f32[1,64,64,128]{3,2,1,0:T(8,128)S(1)}, f32[1,64,64,128]{3,2,1,0:T(8,128)}, u32[]{:S(2)}) copy-start(f32[1,64,64,128]{3,2,1,0:T(8,128)} %param.13) | copy-start | bytes 6291460
  0.6 25.3 %copy-start.6 = (s32[1,64]{1,0:T(1,128)S(1)}, s32[1,64]{1,0:T(1,128)}, u32[]{:S(2)}) copy-start(s32[1,64]{1,0:T(1,128)} %param.17) | copy-start | bytes 772
  1.5 30.8 %collective-permute-start.2 = (f32[1,256]{1,0:T(1,128)S(1)}, f32[1,256]{1,0:T(1,128)S(1)}, u32[]{:S(2)}, u32[]{:S(2)}) collective-permute-start(f32[1,256]{1,0:T(1,128)S(1)} %get-tuple-element.72), channel_id=1, source_target_pairs={{4,0},{8,4},{12,8},{16,12},{20,16},{24,20},{28,24},{32,28},{36,32}... | collective-permute-start | bytes 3080 | tf_op jit(solution)/shard_map/ppermute | solution.py:20
  6.7 25.7 %collective-permute-start = (f32[1,256]{1,0:T(1,128)S(1)}, f32[1,256]{1,0:T(1,128)S(1)}, u32[]{:S(2)}, u32[]{:S(2)}) collective-permute-start(f32[1,256]{1,0:T(1,128)S(1)} %get-tuple-element.73), channel_id=1, source_target_pairs={{0,4},{4,8},{8,12},{12,16},{16,20},{20,24},{24,28},{28,32},{32,36}... | collective-permute-start | bytes 3080 | tf_op jit(solution)/shard_map/ppermute | solution.py:19
  9.3 18.6 %collective-permute-start.1 = (f32[1,256]{1,0:T(1,128)S(1)}, f32[1,256]{1,0:T(1,128)S(1)}, u32[]{:S(2)}, u32[]{:S(2)}) collective-permute-start(f32[1,256]{1,0:T(1,128)S(1)} %get-tuple-element.74), channel_id=1, source_target_pairs={{0,4},{4,8},{8,12},{12,16},{16,20},{20,24},{24,28},{28,32},{32,36}... | collective-permute-start | bytes 3080 | tf_op jit(solution)/shard_map/ppermute | solution.py:19
  11.5 16.4 %collective-permute-start.3 = (f32[1,256]{1,0:T(1,128)S(1)}, f32[1,256]{1,0:T(1,128)S(1)}, u32[]{:S(2)}, u32[]{:S(2)}) collective-permute-start(f32[1,256]{1,0:T(1,128)S(1)} %get-tuple-element.75), channel_id=1, source_target_pairs={{4,0},{8,4},{12,8},{16,12},{20,16},{24,20},{28,24},{32,28},{36,32}... | collective-permute-start | bytes 3080 | tf_op jit(solution)/shard_map/ppermute | solution.py:20
  17.9 21.6 %copy-start.2 = (f32[64,256]{1,0:T(8,128)S(1)}, f32[64,256]{1,0:T(8,128)}, u32[]{:S(2)}) copy-start(f32[64,256]{1,0:T(8,128)} %param.12) | copy-start | bytes 196612
  28.0 10.5 %collective-permute-start.5 = (f32[66,1]{1,0:T(8,128)S(1)}, f32[66,1]{1,0:T(8,128)S(1)}, u32[]{:S(2)}, u32[]{:S(2)}) collective-permute-start(f32[66,1]{1,0:T(8,128)S(1)} %get-tuple-element.60), channel_id=1, source_target_pairs={{0,1},{1,2},{2,3},{4,5},{5,6},{6,7},{8,9},{9,10},{10,11},{12,13},{... | collective-permute-start | bytes 800 | tf_op jit(solution)/shard_map/ppermute | solution.py:19
  31.0 7.5 %collective-permute-start.7 = (f32[66,1]{1,0:T(8,128)S(1)}, f32[66,1]{1,0:T(8,128)S(1)}, u32[]{:S(2)}, u32[]{:S(2)}) collective-permute-start(f32[66,1]{1,0:T(8,128)S(1)} %get-tuple-element.61), channel_id=1, source_target_pairs={{1,0},{2,1},{3,2},{5,4},{6,5},{7,6},{9,8},{10,9},{11,10},{13,12},{... | collective-permute-start | bytes 800 | tf_op jit(solution)/shard_map/ppermute | solution.py:20
  32.5 6.1 %collective-permute-start.6 = (f32[66,1]{1,0:T(8,128)S(1)}, f32[66,1]{1,0:T(8,128)S(1)}, u32[]{:S(2)}, u32[]{:S(2)}) collective-permute-start(f32[66,1]{1,0:T(8,128)S(1)} %get-tuple-element.58), channel_id=1, source_target_pairs={{1,0},{2,1},{3,2},{5,4},{6,5},{7,6},{9,8},{10,9},{11,10},{13,12},{... | collective-permute-start | bytes 800 | tf_op jit(solution)/shard_map/ppermute | solution.py:20
  33.7 5.7 %collective-permute-start.4 = (f32[66,1]{1,0:T(8,128)S(1)}, f32[66,1]{1,0:T(8,128)S(1)}, u32[]{:S(2)}, u32[]{:S(2)}) collective-permute-start(f32[66,1]{1,0:T(8,128)S(1)} %get-tuple-element.59), channel_id=1, source_target_pairs={{0,1},{1,2},{2,3},{4,5},{5,6},{6,7},{8,9},{9,10},{10,11},{12,13},{... | collective-permute-start | bytes 800 | tf_op jit(solution)/shard_map/ppermute | solution.py:19
  39.8 7.0 %collective-permute-start.8 = (f32[1,256]{1,0:T(1,128)S(1)}, f32[1,256]{1,0:T(1,128)S(1)}, u32[]{:S(2)}, u32[]{:S(2)}) collective-permute-start(f32[1,256]{1,0:T(1,128)S(1)} %get-tuple-element.70), channel_id=1, source_target_pairs={{0,4},{4,8},{8,12},{12,16},{16,20},{20,24},{24,28},{28,32},{32,36}... | collective-permute-start | bytes 3080 | tf_op jit(solution)/shard_map/ppermute | solution.py:19
  44.8 4.9 %collective-permute-start.9 = (f32[1,256]{1,0:T(1,128)S(1)}, f32[1,256]{1,0:T(1,128)S(1)}, u32[]{:S(2)}, u32[]{:S(2)}) collective-permute-start(f32[1,256]{1,0:T(1,128)S(1)} %get-tuple-element.71), channel_id=1, source_target_pairs={{4,0},{8,4},{12,8},{16,12},{20,16},{24,20},{28,24},{32,28},{36,32}... | collective-permute-start | bytes 3080 | tf_op jit(solution)/shard_map/ppermute | solution.py:20
  49.8 5.3 %collective-permute-start.10 = (f32[66,1]{1,0:T(8,128)S(1)}, f32[66,1]{1,0:T(8,128)S(1)}, u32[]{:S(2)}, u32[]{:S(2)}) collective-permute-start(f32[66,1]{1,0:T(8,128)S(1)} %get-tuple-element.56), channel_id=1, source_target_pairs={{0,1},{1,2},{2,3},{4,5},{5,6},{6,7},{8,9},{9,10},{10,11},{12,13},{... | collective-permute-start | bytes 800 | tf_op jit(solution)/shard_map/ppermute | solution.py:19
  53.8 5.0 %collective-permute-start.11 = (f32[66,1]{1,0:T(8,128)S(1)}, f32[66,1]{1,0:T(8,128)S(1)}, u32[]{:S(2)}, u32[]{:S(2)}) collective-permute-start(f32[66,1]{1,0:T(8,128)S(1)} %get-tuple-element.57), channel_id=1, source_target_pairs={{1,0},{2,1},{3,2},{5,4},{6,5},{7,6},{9,8},{10,9},{11,10},{13,12},{... | collective-permute-start | bytes 800 | tf_op jit(solution)/shard_map/ppermute | solution.py:20
  59.0 5.3 %collective-permute-start.12 = (f32[1,256]{1,0:T(1,128)S(1)}, f32[1,256]{1,0:T(1,128)S(1)}, u32[]{:S(2)}, u32[]{:S(2)}) collective-permute-start(f32[1,256]{1,0:T(1,128)S(1)} %get-tuple-element.68), channel_id=1, source_target_pairs={{0,4},{4,8},{8,12},{12,16},{16,20},{20,24},{24,28},{28,32},{32,36}... | collective-permute-start | bytes 3080 | tf_op jit(solution)/shard_map/ppermute | solution.py:19
  62.1 4.9 %collective-permute-start.13 = (f32[1,256]{1,0:T(1,128)S(1)}, f32[1,256]{1,0:T(1,128)S(1)}, u32[]{:S(2)}, u32[]{:S(2)}) collective-permute-start(f32[1,256]{1,0:T(1,128)S(1)} %get-tuple-element.69), channel_id=1, source_target_pairs={{4,0},{8,4},{12,8},{16,12},{20,16},{24,20},{28,24},{32,28},{36,32}... | collective-permute-start | bytes 3080 | tf_op jit(solution)/shard_map/ppermute | solution.py:20
  67.1 5.0 %collective-permute-start.14 = (f32[66,1]{1,0:T(8,128)S(1)}, f32[66,1]{1,0:T(8,128)S(1)}, u32[]{:S(2)}, u32[]{:S(2)}) collective-permute-start(f32[66,1]{1,0:T(8,128)S(1)} %get-tuple-element.54), channel_id=1, source_target_pairs={{0,1},{1,2},{2,3},{4,5},{5,6},{6,7},{8,9},{9,10},{10,11},{12,13},{... | collective-permute-start | bytes 800 | tf_op jit(solution)/shard_map/ppermute | solution.py:19
  70.7 4.7 %collective-permute-start.15 = (f32[66,1]{1,0:T(8,128)S(1)}, f32[66,1]{1,0:T(8,128)S(1)}, u32[]{:S(2)}, u32[]{:S(2)}) collective-permute-start(f32[66,1]{1,0:T(8,128)S(1)} %get-tuple-element.55), channel_id=1, source_target_pairs={{1,0},{2,1},{3,2},{5,4},{6,5},{7,6},{9,8},{10,9},{11,10},{13,12},{... | collective-permute-start | bytes 800 | tf_op jit(solution)/shard_map/ppermute | solution.py:20
  75.6 5.7 %collective-permute-start.16 = (f32[1,256]{1,0:T(1,128)S(1)}, f32[1,256]{1,0:T(1,128)S(1)}, u32[]{:S(2)}, u32[]{:S(2)}) collective-permute-start(f32[1,256]{1,0:T(1,128)S(1)} %get-tuple-element.66), channel_id=1, source_target_pairs={{0,4},{4,8},{8,12},{12,16},{16,20},{20,24},{24,28},{28,32},{32,36}... | collective-permute-start | bytes 3080 | tf_op jit(solution)/shard_map/ppermute | solution.py:19
  79.3 4.9 %collective-permute-start.17 = (f32[1,256]{1,0:T(1,128)S(1)}, f32[1,256]{1,0:T(1,128)S(1)}, u32[]{:S(2)}, u32[]{:S(2)}) collective-permute-start(f32[1,256]{1,0:T(1,128)S(1)} %get-tuple-element.67), channel_id=1, source_target_pairs={{4,0},{8,4},{12,8},{16,12},{20,16},{24,20},{28,24},{32,28},{36,32}... | collective-permute-start | bytes 3080 | tf_op jit(solution)/shard_map/ppermute | solution.py:20
  84.3 4.8 %collective-permute-start.18 = (f32[66,1]{1,0:T(8,128)S(1)}, f32[66,1]{1,0:T(8,128)S(1)}, u32[]{:S(2)}, u32[]{:S(2)}) collective-permute-start(f32[66,1]{1,0:T(8,128)S(1)} %get-tuple-element.52), channel_id=1, source_target_pairs={{0,1},{1,2},{2,3},{4,5},{5,6},{6,7},{8,9},{9,10},{10,11},{12,13},{... | collective-permute-start | bytes 800 | tf_op jit(solution)/shard_map/ppermute | solution.py:19
  87.5 4.7 %collective-permute-start.19 = (f32[66,1]{1,0:T(8,128)S(1)}, f32[66,1]{1,0:T(8,128)S(1)}, u32[]{:S(2)}, u32[]{:S(2)}) collective-permute-start(f32[66,1]{1,0:T(8,128)S(1)} %get-tuple-element.53), channel_id=1, source_target_pairs={{1,0},{2,1},{3,2},{5,4},{6,5},{7,6},{9,8},{10,9},{11,10},{13,12},{... | collective-permute-start | bytes 800 | tf_op jit(solution)/shard_map/ppermute | solution.py:20
  92.5 6.4 %collective-permute-start.20 = (f32[1,256]{1,0:T(1,128)S(1)}, f32[1,256]{1,0:T(1,128)S(1)}, u32[]{:S(2)}, u32[]{:S(2)}) collective-permute-start(f32[1,256]{1,0:T(1,128)S(1)} %get-tuple-element.64), channel_id=1, source_target_pairs={{0,4},{4,8},{8,12},{12,16},{16,20},{20,24},{24,28},{28,32},{32,36}... | collective-permute-start | bytes 3080 | tf_op jit(solution)/shard_map/ppermute | solution.py:19
  97.0 4.9 %collective-permute-start.21 = (f32[1,256]{1,0:T(1,128)S(1)}, f32[1,256]{1,0:T(1,128)S(1)}, u32[]{:S(2)}, u32[]{:S(2)}) collective-permute-start(f32[1,256]{1,0:T(1,128)S(1)} %get-tuple-element.65), channel_id=1, source_target_pairs={{4,0},{8,4},{12,8},{16,12},{20,16},{24,20},{28,24},{32,28},{36,32}... | collective-permute-start | bytes 3080 | tf_op jit(solution)/shard_map/ppermute | solution.py:20
  102.0 3.4 collective-permute-start.22
  103.6 4.7 %collective-permute-start.23 = (f32[66,1]{1,0:T(8,128)S(1)}, f32[66,1]{1,0:T(8,128)S(1)}, u32[]{:S(2)}, u32[]{:S(2)}) collective-permute-start(f32[66,1]{1,0:T(8,128)S(1)} %get-tuple-element.51), channel_id=1, source_target_pairs={{1,0},{2,1},{3,2},{5,4},{6,5},{7,6},{9,8},{10,9},{11,10},{13,12},{... | collective-permute-start | bytes 800 | tf_op jit(solution)/shard_map/ppermute | solution.py:20
  123.7 211.1 %all-to-all-start = ((f32[64,4,64,128]{3,2,1,0:T(8,128)}), f32[64,4,64,128]{3,2,1,0:T(8,128)}, u32[]{:S(2)}, u32[]{:S(2)}) async-start(f32[64,4,64,128]{3,2,1,0:T(8,128)} %copy.54), calls=%async_computation | async-start | bytes 16777216 | tf_op jit(solution)/shard_map/all_to_all | solution.py:110
  145.0 178.4 %collective-permute-start.24 = (f32[1,256]{1,0:T(1,128)S(1)}, f32[1,256]{1,0:T(1,128)S(1)}, u32[]{:S(2)}, u32[]{:S(2)}) collective-permute-start(f32[1,256]{1,0:T(1,128)S(1)} %get-tuple-element.62), channel_id=1, source_target_pairs={{0,4},{4,8},{8,12},{12,16},{16,20},{20,24},{24,28},{28,32},{32,36}... | collective-permute-start | bytes 3080 | tf_op jit(solution)/shard_map/ppermute | solution.py:19
  148.6 178.7 %collective-permute-start.25 = (f32[1,256]{1,0:T(1,128)S(1)}, f32[1,256]{1,0:T(1,128)S(1)}, u32[]{:S(2)}, u32[]{:S(2)}) collective-permute-start(f32[1,256]{1,0:T(1,128)S(1)} %get-tuple-element.63), channel_id=1, source_target_pairs={{4,0},{8,4},{12,8},{16,12},{20,16},{24,20},{28,24},{32,28},{36,32}... | collective-permute-start | bytes 3080 | tf_op jit(solution)/shard_map/ppermute | solution.py:20
  327.4 3.2 collective-permute-start.26
  329.3 4.7 %collective-permute-start.27 = (f32[66,1]{1,0:T(8,128)S(1)}, f32[66,1]{1,0:T(8,128)S(1)}, u32[]{:S(2)}, u32[]{:S(2)}) collective-permute-start(f32[66,1]{1,0:T(8,128)S(1)} %get-tuple-element.49), channel_id=1, source_target_pairs={{1,0},{2,1},{3,2},{5,4},{6,5},{7,6},{9,8},{10,9},{11,10},{13,12},{... | collective-permute-start | bytes 800 | tf_op jit(solution)/shard_map/ppermute | solution.py:20
  (4 other events, 56.5 us)
where the time goes:
time: 368 us; the launch traced here: 366 us
  waiting for transfers between devices  205 us (56%)
  starting transfers between devices  93 us (25%)
  local copies, waits for them, and re-layouts  39.3 us (11%)
  matrix products  16.3 us (4%)
  other arithmetic  8.18 us (2%)
  between operations  4.11 us (1%)
    ppermute x14, waiting for transfers between devices, with_halo(): before = lax.ppermute(last, axis, up)  174 us
    ppermute x14, starting transfers between devices, with_halo(): before = lax.ppermute(last, axis, up)  45.8 us
    ppermute x14, waiting for transfers between devices, with_halo(): after = lax.ppermute(initial, axis, down)  31.8 us
    ppermute x14, starting transfers between devices, with_halo(): after = lax.ppermute(initial, axis, down)  26.1 us
    all_to_all x1, starting transfers between devices, shards(): lax.all_to_all(outgoing, 'slab', split_axis=0, concat_axis=0, tiled=True)  21.1 us
    unnamed x17, local copies, waits for them, and re-layouts  16.5 us
    dot_general x1, local copies, waits for them, and re-layouts, shards(): jnp.dot(take, arrived.reshape(slab_count * CAP, -1), precision=HI)  9.04 us
    dot_general x1, local copies, waits for them, and re-layouts, shards(): jnp.dot(pick, final.reshape(old_slots, -1), precision=HI)  8.13 us
  transfers between devices with their start and end apart: 29, of which 12 were waited for; matrix products, arithmetic and copies ran while one was open for 4% of the time, Pallas kernels for 0%

commit v1 on v0

v1 whole, which is shorter than its diff:
```python
import functools

import jax
import jax.numpy as jnp
from jax import lax
from jax.experimental import pallas as pl
from jax.experimental.pallas import tpu as pltpu
from jax.sharding import PartitionSpec as P

MESH = pl.DeviceIdType.MESH
HI = lax.Precision.HIGHEST
F32, I32 = jnp.float32, jnp.int32
SLABS = 64
CHIPS = 32
SH = 64
NEW = 32
OLD = 64
STEPS, ITERS = 2, 3
IDX2, IDX3 = 16, 24


def iota(shape, dim):
    return lax.broadcasted_iota(I32, shape, dim)


def strict_upper(n):
    return (iota((n, n), 0) < iota((n, n), 1)).astype(F32)


def route(own, tab, out_ref):
    chip, local = tab >> 7, tab & 63
    n_of, lane32 = iota((NEW, 128), 0), iota((NEW, 128), 1)
    rank = jnp.zeros((NEW, 128), I32)
    for k in range(1, NEW):
        rank = rank + ((pltpu.roll(chip, k, 0) == chip) & (n_of >= k)).astype(I32)
    s_of = n_of
    feeds = jnp.zeros((CHIPS, 128), jnp.bool_)
    for n in range(NEW):
        feeds = feeds | (s_of == chip[n : n + 1, :])
    feeds_f = feeds.astype(F32)
    upper = strict_upper(128)
    group = jnp.dot((iota((CHIPS, CHIPS), 0) > iota((CHIPS, CHIPS), 1)).astype(F32), feeds_f).astype(I32)
    turn = jnp.dot(feeds_f, upper).astype(I32)
    place = ((turn & 7) << 7) + ((turn >> 3) << 5) + s_of
    both = jnp.where(feeds, (place << 6) + s_of, 0)
    rows = [jnp.sum(jnp.where(group == g, both, 0), axis=0, keepdims=True) for g in range(8)]
    both = jnp.concatenate(rows, axis=0)
    to_s, src = both >> 6, both & 63
    packed = jnp.where(feeds, turn * 8 + group + 1, 0).astype(F32)
    turned = jnp.transpose(jnp.concatenate([packed] * 4, axis=0)).astype(I32) - 1
    d_of, l_of = iota((128, 128), 0), iota((128, 128), 1)
    want = jnp.where(turned >= 0, (turned >> 3) - 8 * (l_of >> 5), -1)
    code = ((turned & 7) << 7) + d_of
    rows = [jnp.sum(jnp.where(want == q, code, 0), axis=0, keepdims=True) for q in range(8)]
    to_d = jnp.concatenate(rows, axis=0)

    row8, lane8 = iota((8, 128), 0), iota((8, 128), 1)
    here = (row8 << 7) + lane8

    def look(table, at):
        row, lane = at >> 7, at & 127
        out = jnp.zeros((8, 128), I32)
        for r in range(8):
            line = jnp.broadcast_to(table[r : r + 1, :], (8, 128))
            out = jnp.where(row == r, jnp.take_along_axis(line, lane, axis=1), out)
        return out

    def flip(x, k):
        for bit in (1, 2, 4):
            if k & bit:
                x = jnp.where((row8 & bit) == 0, pltpu.roll(x, 8 - bit, 0), pltpu.roll(x, bit, 0))
        return x

    def mate(x, colour, level):
        out = flip(x, level)
        for k in range(level + 1, 2 * level):
            out = jnp.where(flip(colour, k) == colour, flip(x, k), out)
        return out

    colour = jnp.zeros((8, 128), I32)
    for level, doublings in ((1, 8), (2, 7), (4, 6)):
        colour_s = look(colour, to_d) if level > 1 else colour
        partner = mate(here, colour_s, level)
        back = look(to_d, look(partner, to_s) if level > 1 else to_s ^ 128)
        hop = mate(back, colour, level)
        label = here
        for _ in range(doublings):
            got = look((hop << 10) + label, hop)
            label = jnp.minimum(label, got & 1023)
            hop = got >> 10
        colour = colour * 2 + (label > mate(label, colour, level)).astype(I32)

    colour_sd = jnp.zeros((CHIPS, 128), I32)
    colour_nd = jnp.zeros((NEW, 128), I32)
    for g in range(8):
        line, of = colour[g : g + 1, :], src[g : g + 1, :]
        colour_sd = colour_sd + jnp.where(s_of == of, line, 0)
        colour_nd = colour_nd + jnp.where(chip == of, line, 0)
    colour_sd = jnp.where(feeds, colour_sd, -1)
    masks = jnp.concatenate([(colour_sd == c).astype(F32) for c in range(8)], axis=0)
    counts = jnp.dot(masks, upper) * masks
    half = counts[0:CHIPS]
    for c in range(1, 8):
        half = half + counts[c * CHIPS : (c + 1) * CHIPS]
    half = half.astype(I32)
    own_chip = own >> 1
    mine = chip == own_chip
    slots = [
        jnp.sum(jnp.where(mine & (rank == r), local, 0), axis=0, keepdims=True) for r in range(4)
    ]
    slots = jnp.concatenate(slots + [jnp.zeros((4, 128), I32)], axis=0).astype(F32)
    own_row = s_of == own_chip
    colour_s = jnp.sum(jnp.where(own_row, colour_sd, 0), axis=0, keepdims=True)
    half_s = jnp.sum(jnp.where(own_row, half, 0), axis=0, keepdims=True)
    for h in range(2):
        pick = ((row8 == colour_s) & (half_s == h)).astype(F32)
        got = lax.dot_general(pick, slots, (((1,), (1,)), ((), ())), preferred_element_type=F32)
        out_ref[8 * h : 8 * h + 8, 0:8] = got.astype(I32)
    take = jnp.sum(jnp.where(colour_sd == own_chip >> 2, 2 * s_of + half, 0), axis=0, keepdims=True)
    out_ref[IDX2 : IDX2 + 8, :] = jnp.broadcast_to(take, (8, 128))
    via = colour_nd * 4 + rank
    via = jnp.sum(jnp.where(lane32 == own, via, 0), axis=1, keepdims=True)
    out_ref[IDX3 : IDX3 + NEW, :] = jnp.broadcast_to(via, (NEW, 128))


def matrices(cap_row, trans_row, out_ref):
    shape = (SH, 128)
    k_of, lane = iota(shape, 0), iota(shape, 1)
    eye = k_of == lane

    def column(row):
        return jnp.broadcast_to(jnp.sum(jnp.where(eye, row, 0.0), axis=1, keepdims=True), shape)

    cap, tr = column(cap_row), column(trans_row)
    inner = jnp.where(k_of == SH - 1, 0.0, pltpu.roll(tr, SH - 1, 0))
    t0 = jnp.broadcast_to(trans_row[:, 0:1], shape)
    b = cap + tr + inner
    c = -inner
    a = jnp.where(k_of == 0, 0.0, -tr)
    rhs = eye.astype(F32)
    s = 1
    while s < SH:
        up, down = (lambda x: pltpu.roll(x, s, 0)), (lambda x: pltpu.roll(x, SH - s, 0))
        al, ga = -a / up(b), -c / down(b)
        rhs = rhs + al * up(rhs) + ga * down(rhs)
        b = b + al * up(c) + ga * down(a)
        a, c = al * up(a), ga * down(c)
        s *= 2
    inverse = rhs / b
    amat = inverse * cap_row
    couple = jnp.broadcast_to(inverse[:, 0:1], shape) * t0
    asq = jnp.dot(amat[:, :SH], amat, precision=HI, preferred_element_type=F32)
    acouple = jnp.dot(amat[:, :SH], couple, precision=HI, preferred_element_type=F32)
    out_ref[0] = asq
    out_ref[1] = t0 * column(amat[0:1, :])
    out_ref[2] = t0 * column(asq[0:1, :])
    out_ref[3] = acouple
    out_ref[4] = couple
    out_ref[5, 0:8, :] = t0[0:8] * (1.0 - jnp.broadcast_to(couple[0:1], (8, 128)))
    out_ref[5, 8:16, :] = t0[0:8] * jnp.broadcast_to(acouple[0:1], (8, 128))


def prepare_kernel(own_of, tab_ref, cap_ref, trans_ref, tbl_ref, mat_ref):
    matrices(cap_ref[...], trans_ref[...], mat_ref)
    route(own_of(), tab_ref[...], tbl_ref)


def prepare(own_of, table, cap, tr, **more):
    tab = jnp.pad(table.reshape(SLABS, NEW).T, ((0, 0), (0, 128 - SLABS)), constant_values=-1)
    pad = lambda x: jnp.pad(x, (0, 128 - SH)).reshape(1, 128)
    return pl.pallas_call(
        functools.partial(prepare_kernel, own_of),
        out_shape=(jax.ShapeDtypeStruct((56, 128), I32), jax.ShapeDtypeStruct((6, SH, 128), F32)),
        in_specs=[pl.BlockSpec(memory_space=pltpu.VMEM)] * 3,
        out_specs=[pl.BlockSpec(memory_space=pltpu.VMEM)] * 2,
        **more,
    )(tab, pad(cap), pad(tr))


WIDE = 8
DEFAULTS = (1.0, 1.0, 0.0, 0.0, 0.0, 0.0, 0.0)
NF = len(DEFAULTS)
HALO = 2 * WIDE


def move_kernel(
    slabs, cols,
    tbl, p_ref, storage_ref, trans_ref, source_ref, old_ref, cb_ref, mat_ref,
    p_out, new_out,
    field, rows_in, edge_l, edge_r, from_l, from_r, line1, line2, shells1, shells2,
    stage1, mid, stage2, got, pb_stage, pb_mid,
    halo_send, halo_recv, send1, recv1, send_pb, recv_pb, send2, recv2,
):
    own, col = lax.axis_index("slab"), lax.axis_index("col")
    chip = own // 2
    first_core, second_core = own % 2 == 0, own % 2 == 1
    neighbours = []
    for dr, dc in ((-1, 0), (1, 0), (0, -1), (0, 1), (-1, -1), (1, -1), (-1, 1), (1, 1)):
        ok = None
        for step, at, size in ((dr, own, slabs), (dc, col, cols)):
            if step:
                inside = at > 0 if step < 0 else at < size - 1
                ok = inside if ok is None else ok & inside
        neighbours.append((ok, dr, dc))

    lane80 = iota((80, 128), 1)
    for f, value in enumerate(DEFAULTS):
        rows_in[f] = jnp.full((HALO, 256), value, F32)
    default = jnp.full((80, 128), 0.0, F32)
    for f, value in enumerate(DEFAULTS):
        if value:
            default = jnp.where(lane80 // WIDE == f, value, default)
    from_l[...] = default
    from_r[...] = default

    barrier = pltpu.get_barrier_semaphore()

    def greet(slab, c):
        pl.semaphore_signal(barrier, inc=1, device_id={"slab": slab, "col": c}, device_id_type=MESH)

    for ok, dr, dc in neighbours:
        if dc:
            @pl.when(ok)
            def _():
                greet(own + dr, col + dc)

    @pl.when(first_core)
    def _():
        def body(k, _):
            greet(2 * ((chip + k) % CHIPS) + 1, col)
            return 0
        lax.fori_loop(0, CHIPS, body, 0)

    @pl.when(second_core)
    def _():
        def body(k, _):
            greet((own + k) % slabs, col)
            return 0
        lax.fori_loop(1, slabs, body, 0)

    weight1, weight2 = mat_ref[1], mat_ref[2]

    @pl.when(first_core)
    def _():
        def body(o, _):
            x = old_ref[o]
            shells1[pl.ds(o, 1), :] = jnp.sum(x * weight1, axis=0, keepdims=True)
            shells2[pl.ds(o, 1), :] = jnp.sum(x * weight2, axis=0, keepdims=True)
            return 0
        lax.fori_loop(0, OLD, body, 0)

    row64 = iota((64, 64), 0)
    blocks = cb_ref[...]
    hot = [(blocks == 2 * row64 + h).astype(F32) for h in range(2)]
    field[0] = p_ref[...]
    field[1] = storage_ref[...]
    field[2] = trans_ref[...]
    field[3] = source_ref[...]

    @pl.when(first_core)
    def _():
        for h in range(2):
            part = pl.ds(128 * h, 128)
            field[4, :, part] = jnp.dot(hot[h], shells1[...], precision=HI, preferred_element_type=F32)
            field[5, :, part] = jnp.dot(hot[h], shells2[...], precision=HI, preferred_element_type=F32)
            field[6, :, part] = jnp.broadcast_to(jnp.sum(hot[h], axis=1, keepdims=True), (64, 128))

    @pl.when(second_core)
    def _():
        for f in range(4, 7):
            field[f] = jnp.zeros((64, 256), F32)

    lane64 = iota((64, 128), 1)
    left, right = jnp.zeros((64, 128), F32), jnp.zeros((64, 128), F32)
    for f in range(NF):
        spot = lane64 // WIDE == f
        a, b = field[f, :, 0:128], field[f, :, 128:256]
        left = jnp.where(spot, pltpu.roll(a, WIDE * f, 1) if f else a, left)
        right = jnp.where(spot, pltpu.roll(b, WIDE * (f + 1), 1), right)
    edge_l[...] = left
    edge_r[...] = right

    extra = (col > 0).astype(I32) + (col < cols - 1).astype(I32)
    near = 1 + (own > 0).astype(I32) + (own < slabs - 1).astype(I32)
    pl.semaphore_wait(barrier, extra * near + jnp.where(first_core, CHIPS, slabs - 1))

    def copy_of(i, dr, dc):
        if dc == 0:
            src = field.at[:, pl.ds(0 if dr < 0 else 64 - WIDE, WIDE), :]
            dst = rows_in.at[:, pl.ds(WIDE if dr > 0 else 0, WIDE), :]
        else:
            src, dst = (edge_l, from_r) if dc < 0 else (edge_r, from_l)
            if dr == 0:
                dst = dst.at[pl.ds(0, 64), :]
            else:
                src = src.at[pl.ds(0 if dr < 0 else 64 - WIDE, WIDE), :]
                dst = dst.at[pl.ds(64 + (WIDE if dr > 0 else 0), WIDE), :]
        return pltpu.make_async_remote_copy(
            src_ref=src, dst_ref=dst, send_sem=halo_send.at[i], recv_sem=halo_recv.at[i],
            device_id={"slab": own + dr, "col": col + dc}, device_id_type=MESH,
        )

    for i, (ok, dr, dc) in enumerate(neighbours):
        @pl.when(ok)
        def _():
            copy_of(i, dr, dc).start()

    def to_middle(src, dst, send, recv, m):
        return pltpu.make_async_remote_copy(
            src_ref=src, dst_ref=dst, send_sem=send, recv_sem=recv,
            device_id={"slab": 2 * m + 1}, device_id_type=MESH,
        )

    @pl.when(first_core)
    def _():
        square = mat_ref[0][:, :SH]

        def body(k, _):
            m = (chip + k) % CHIPS
            for h in range(2):
                slot = tbl[8 * h + m // 4, m % 4]
                stage1[2 * m + h] = jnp.dot(square, old_ref[slot], precision=HI, preferred_element_type=F32)
            to_middle(stage1.at[pl.ds(2 * m, 2)], mid.at[pl.ds(2 * chip, 2)], send1, recv1, m).start()
            return 0
        lax.fori_loop(0, CHIPS, body, 0)

    for i, (ok, dr, dc) in enumerate(neighbours):
        back = next(b for b, n in enumerate(neighbours) if n[1:] == (-dr, -dc))
        @pl.when(neighbours[back][0])
        def _():
            copy_of(i, dr, dc).wait_recv()

    shape = (64 + HALO, 384)
    in_l, in_r = from_l[...], from_r[...]

    def extended(f):
        rows = jnp.concatenate([field[f], rows_in[f]], axis=0)
        tail = jnp.where(lane80 >= 128 - WIDE, pltpu.roll(in_l, (128 - WIDE * (f + 1)) % 128, 1), DEFAULTS[f])
        tail = jnp.where(lane80 < WIDE, pltpu.roll(in_r, (128 - WIDE * f) % 128, 1), tail)
        return jnp.concatenate([rows, tail], axis=1)

    def after(x, axis):
        return pltpu.roll(x, shape[axis] - 1, axis)

    def before(x, axis):
        return pltpu.roll(x, 1, axis)

    p, storage, trans, source, base1, base2, active = [extended(f) for f in range(NF)]
    kappa, cross = mat_ref[5, 0:1, 0:1], mat_ref[5, 8:9, 0:1]
    faces = []
    for axis in (1, 0):
        other = after(trans, axis)
        total = trans + other
        faces.append(2.0 * trans * other / jnp.where(total == 0.0, 1.0, total))
    conduct = faces[0] + before(faces[0], 1) + faces[1] + before(faces[1], 0)
    draw = active * kappa
    slope0 = storage + draw
    half = [0.5 * x for x in faces]
    base = base1
    for step, line in ((0, line1), (1, line2)):
        prev = p
        for sweep in range(ITERS):
            if sweep == ITERS - 1:
                line[...] = p[0:64, 0:256]
                if step == 0:
                    base = base2 + active * (cross * p)
            flux = jnp.zeros(shape, F32)
            for axis, face in zip((1, 0), half):
                other = after(p, axis)
                flow = face * (other + p) * (other - p)
                flux = flux + flow - before(flow, axis)
            misfit = storage * (p - prev) - flux + (draw * p - (base1 if step == 0 else base)) - source
            p = p - misfit / (slope0 + p * conduct)
    p_out[...] = p[0:64, 0:256]

    @pl.when(first_core)
    def _():
        for line, rows in ((line1, shells1), (line2, shells2)):
            total = jnp.zeros((OLD, 128), F32)
            for h in range(2):
                total = total + lax.dot_general(
                    hot[h], line[:, 128 * h : 128 * h + 128], (((0,), (0,)), ((), ())),
                    precision=HI, preferred_element_type=F32,
                )
            rows[...] = total

        def body(k, _):
            m = (chip + k) % CHIPS
            for h in range(2):
                slot = tbl[8 * h + m // 4, m % 4]
                pb_stage[m, pl.ds(h, 1), :] = shells1[pl.ds(slot, 1), :]
                pb_stage[m, pl.ds(2 + h, 1), :] = shells2[pl.ds(slot, 1), :]
            for r in range(4, 8):
                pb_stage[m, pl.ds(r, 1), :] = jnp.zeros((1, 128), F32)
            to_middle(pb_stage.at[m], pb_mid.at[chip], send_pb, recv_pb, m).start()
            return 0
        lax.fori_loop(0, CHIPS, body, 0)

    def await_bytes(ref, sem):
        pltpu.make_async_copy(ref, ref, sem).wait()

    @pl.when(second_core)
    def _():
        await_bytes(mid, recv1)
        await_bytes(pb_mid, recv_pb)
        acouple, couple = mat_ref[3], mat_ref[4]

        def block(d):
            i = tbl[IDX2, d]
            s, h = i // 2, i % 2
            first = pb_mid[s, pl.ds(h, 1), :]
            second = pb_mid[s, pl.ds(2 + h, 1), :]
            return mid[i] + acouple * first + couple * second

        def body(k, _):
            d = (own + k) % slabs
            stage2[d] = block(d)
            pltpu.make_async_remote_copy(
                src_ref=stage2.at[d], dst_ref=got.at[chip], send_sem=send2, recv_sem=recv2,
                device_id={"slab": d}, device_id_type=MESH,
            ).start()
            return 0
        lax.fori_loop(1, slabs, body, 0)
        got[chip] = block(own)
        await_bytes(got.at[pl.ds(0, CHIPS - 1)], recv2)

    @pl.when(first_core)
    def _():
        await_bytes(got, recv2)

    def gather(n, _):
        new_out[n] = got[tbl[IDX3 + n, 0]]
        return 0
    lax.fori_loop(0, NEW, gather, 0)

    for i, (ok, dr, dc) in enumerate(neighbours):
        @pl.when(ok)
        def _():
            copy_of(i, dr, dc).wait_send()

    @pl.when(first_core)
    def _():
        await_bytes(stage1, send1)
        await_bytes(pb_stage, send_pb)

    @pl.when(second_core)
    def _():
        await_bytes(stage2.at[pl.ds(0, 2 * CHIPS - 1)], send2)


def solution(mesh):
    slabs, cols = mesh.shape["slab"], mesh.shape["col"]

    def shards(pressure, storage, trans, source, shells_old, cap, tr, new_source, cell_block):
        table, mats = prepare(lambda: lax.axis_index("slab"), new_source[0], cap, tr)
        vmem = pl.BlockSpec(memory_space=pltpu.VMEM)
        p, new = pl.pallas_call(
            functools.partial(move_kernel, slabs, cols),
            out_shape=(
                jax.ShapeDtypeStruct((64, 256), F32),
                jax.ShapeDtypeStruct((NEW, SH, 128), F32),
            ),
            in_specs=[pl.BlockSpec(memory_space=pltpu.SMEM)] + [vmem] * 7,
            out_specs=[vmem] * 2,
            scratch_shapes=[
                pltpu.VMEM((NF, 64, 256), F32),
                pltpu.VMEM((NF, HALO, 256), F32),
                pltpu.VMEM((64, 128), F32),
                pltpu.VMEM((64, 128), F32),
                pltpu.VMEM((80, 128), F32),
                pltpu.VMEM((80, 128), F32),
                pltpu.VMEM((64, 256), F32),
                pltpu.VMEM((64, 256), F32),
                pltpu.VMEM((OLD, 128), F32),
                pltpu.VMEM((OLD, 128), F32),
                pltpu.VMEM((2 * CHIPS, SH, 128), F32),
                pltpu.VMEM((2 * CHIPS, SH, 128), F32),
                pltpu.VMEM((2 * CHIPS, SH, 128), F32),
                pltpu.VMEM((CHIPS, SH, 128), F32),
                pltpu.VMEM((CHIPS, 8, 128), F32),
                pltpu.VMEM((CHIPS, 8, 128), F32),
                pltpu.SemaphoreType.DMA((8,)),
                pltpu.SemaphoreType.DMA((8,)),
            ] + [pltpu.SemaphoreType.DMA] * 6,
            compiler_params=pltpu.CompilerParams(
                collective_id=0, has_side_effects=True, vmem_limit_bytes=40 << 20
            ),
        )(table, pressure, storage, trans, source, shells_old[0], cell_block, mats)
        return p, new[None]

    f = P("slab", "col")
    return jax.shard_map(
        shards,
        mesh=mesh,
        in_specs=(f, f, f, f, P("col", "slab", None, None), P(), P(), P("col", None), P("col", "slab")),
        out_specs=(f, P("col", "slab", None, None)),
        check_vma=False,
    )
```

time: 368 us -> 85.5 us (0.23)
  waiting for transfers between devices: 205 us -> 0 us
  starting transfers between devices: 93 us -> 0 us
  Pallas kernels: 0 us -> 71.6 us
  local copies, waits for them, and re-layouts: 39.3 us -> 11.4 us
  matrix products: 16.3 us -> 0 us
  other arithmetic: 8.18 us -> 1.36 us
    ppermute x28 -> x0, waiting for transfers between devices: 205 us -> none  [the longest x14 174 us: with_halo(): before = lax.ppermute(last, axis, up)]
    ppermute x28 -> x0, starting transfers between devices: 71.9 us -> none  [the longest x14 45.8 us: with_halo(): before = lax.ppermute(last, axis, up)]
    pallas_call x0 -> x2, Pallas kernels: none -> 71.6 us  [the longest x1 66.9 us: shards(): pl.pallas_call(functools.partial(move_kernel, slabs, cols), out_shape=(ja...]
    all_to_all x1 -> x0, starting transfers between devices: 21.1 us -> none  [shards(): lax.all_to_all(outgoing, 'slab', split_axis=0, concat_axis=0, tiled=True)]
    dot_general x2 -> x0, local copies, waits for them, and re-layouts: 17.2 us -> none  [the longest x1 9.04 us: shards(): jnp.dot(take, arrived.reshape(slab_count * CAP, -1), precision=HI)]
    dot_general x9 -> x0, matrix products: 16.3 us -> none  [the longest x1 6.57 us: shards(): jnp.dot(take, arrived.reshape(slab_count * CAP, -1), precision=HI)]
    unnamed x17 -> x19, local copies, waits for them, and re-layouts: 16.5 us -> 9.39 us
    slice x41 -> x0, local copies, waits for them, and re-layouts: 4.02 us -> none  [the longest x12 1.2 us: with_halo(): last = lax.slice_in_dim(shard, length - width, length, axis=dim)]
  transfers between devices with their start and end apart: 29 -> 0, of which waited for: 12 -> 0; matrix products, arithmetic and copies ran while one was open for 4% -> 0% of each run, Pallas kernels for 0% -> 0%
where the time goes in v1:
time: 85.5 us; the launch traced here: 85 us
  Pallas kernels  71.6 us (84%)
  local copies, waits for them, and re-layouts  11.4 us (13%)
  other arithmetic  1.36 us (2%)
    pallas_call x1, Pallas kernels, shards(): pl.pallas_call(functools.partial(move_kernel, slabs, cols), out_shape=(ja...  66.9 us
    unnamed x19, local copies, waits for them, and re-layouts  9.39 us
    pallas_call x1, Pallas kernels, prepare(): pl.pallas_call(functools.partial(prepare_kernel, own_of), out_shape=(jax....  4.62 us

profile of v1, /device:TPU:1, one launch (start us, length us, event | category | flops | bytes accessed | tf_op | source)
XLA Modules:
  0.0 85.0 jit_solution(4798179578670924763)
XLA Ops:
  0.6 1.2 %pad_bitcast_fusion = (f32[1,128]{1,0:T(1,128)}, f32[1,128]{1,0:T(1,128)}) fusion(f32[64]{0:T(128)} %param.15, f32[64]{0:T(128)} %param.14), kind=kLoop, calls=%fused_computation | loop fusion | bytes 1536 | tf_op jit(solution)/shard_map/reshape | solution.py:170
  1.9 0.5 broadcast.9
  2.4 1.4 %reduce.3 = s32[2048]{0:T(1024)S(1)} reduce(s32[1,2048]{1,0:T(1,128)} %param.16, s32[]{:T(128)} %broadcast.9), dimensions={0}, to_apply=%param.16.reduce_sub_computation.3 | reduce | bytes 16388 | tf_op args[7]
  3.7 0.1 reshape_squeeze.3
  3.8 0.1 copy.11
  3.9 0.6 pad.11.tab_ref
  4.5 4.6 %shard_map.104 = (s32[56,128]{1,0:T(8,128)}, f32[6,64,128]{2,1,0:T(8,128)}) custom-call(s32[32,128]{1,0:T(8,128)} %pad.11.tab_ref, f32[1,128]{1,0:T(1,128)} %get-tuple-element.11.cap_ref, f32[1,128]{1,0:T(1,128)} %get-tuple-element.10.trans_ref), custom_call_target="tpu_custom_call" | custom-call | tf_op jit(solution)/shard_map/pallas_call | solution.py:171
  9.1 0.0 copy-start
  9.1 1.6 %copy-done = f32[1,64,64,128]{3,2,1,0:T(8,128)S(1)} copy-done((f32[1,64,64,128]{3,2,1,0:T(8,128)S(1)}, f32[1,64,64,128]{3,2,1,0:T(8,128)}, u32[]{:S(2)}) %copy-start) | copy-done | bytes 2097176
  10.7 0.0 copy-start.1
  10.7 0.9 %copy-done.1 = f32[6,64,128]{2,1,0:T(8,128)S(1)} copy-done((f32[6,64,128]{2,1,0:T(8,128)S(1)}, f32[6,64,128]{2,1,0:T(8,128)}, u32[]{:S(2)}) %copy-start.1) | copy-done | bytes 196632
  11.6 0.0 copy-start.2
  11.7 0.8 copy-done.2
  12.5 0.0 copy-start.3
  12.5 0.8 copy-done.3
  13.3 0.0 copy-start.4
  13.3 0.8 copy-done.4
  14.2 0.0 copy-start.5
  14.2 0.8 copy-done.5
  15.0 0.0 copy-start.6
  15.0 0.7 copy-done.6
  15.8 0.0 copy-start.7
  15.8 0.7 copy-done.7
  16.4 66.9 %shard_map.105 = (f32[64,256]{1,0:T(8,128)S(1)}, f32[32,64,128]{2,1,0:T(8,128)S(1)}) custom-call(s32[56,128]{1,0:T(8,128)S(1)} %copy-done.6, f32[64,256]{1,0:T(8,128)S(1)} %copy-done.2, f32[64,256]{1,0:T(8,128)S(1)} %copy-done.3, f32[64,256]{1,0:T(8,128)S(1)} %copy-done.4, f32[64,256]{1,0:T(8,128)S(1)} %copy-done.5, f32[64,64,128]{2,1,0:T(8,128)S(1)} %bitcast.7, ...), custom_call_target="tpu_custom_call" | custom-call | tf_op jit(solution)/shard_map/pallas_call | solution.py:457
  83.4 0.6 copy.14
  84.0 1.0 %copy.15 = f32[1,32,64,128]{3,2,1,0:T(8,128)} copy(f32[1,32,64,128]{3,2,1,0:T(8,128)S(1)} %bitcast.8) | data formatting | bytes 2097152
Async XLA Ops:
  9.1 1.6 %copy-start = (f32[1,64,64,128]{3,2,1,0:T(8,128)S(1)}, f32[1,64,64,128]{3,2,1,0:T(8,128)}, u32[]{:S(2)}) copy-start(f32[1,64,64,128]{3,2,1,0:T(8,128)} %param.13) | copy-start | bytes 6291460
  10.7 0.9 %copy-start.1 = (f32[6,64,128]{2,1,0:T(8,128)S(1)}, f32[6,64,128]{2,1,0:T(8,128)}, u32[]{:S(2)}) copy-start(f32[6,64,128]{2,1,0:T(8,128)} %get-tuple-element.7.mat_ref) | copy-start | bytes 589828
  11.6 0.8 copy-start.2
  12.5 0.8 copy-start.3
  13.3 0.8 copy-start.4
  14.2 0.8 copy-start.5
  15.0 0.7 copy-start.6
  15.8 0.7 copy-start.7

commit v2 on v1

--- a/solution.py
+++ b/solution.py
@@ -25,6 +25,19 @@
 
 def strict_upper(n):
     return (iota((n, n), 0) < iota((n, n), 1)).astype(F32)
+
+
+def lane_of(d):
+    return (d & 3) * 16 + (d >> 2)
+
+
+def by_owner(lines):
+    turned = jnp.transpose(jnp.concatenate([lines.astype(F32)] * 8, axis=0)).astype(I32)
+    part = iota((NEW, 128), 1) >> 4
+    tab = jnp.full((NEW, 128), -1, I32)
+    for a in range(4):
+        tab = jnp.where(part == a, turned[NEW * a : NEW * a + NEW, :], tab)
+    return tab
 
 
 def route(own, tab, out_ref):
@@ -115,25 +128,27 @@
     for h in range(2):
         pick = ((row8 == colour_s) & (half_s == h)).astype(F32)
         got = lax.dot_general(pick, slots, (((1,), (1,)), ((), ())), preferred_element_type=F32)
-        out_ref[8 * h : 8 * h + 8, 0:8] = got.astype(I32)
+        out_ref[8 * h : 8 * h + 8, 0:8] = got.astype(I32) & (OLD - 1)
     take = jnp.sum(jnp.where(colour_sd == own_chip >> 2, 2 * s_of + half, 0), axis=0, keepdims=True)
-    out_ref[IDX2 : IDX2 + 8, :] = jnp.broadcast_to(take, (8, 128))
+    out_ref[IDX2 : IDX2 + 8, :] = jnp.broadcast_to(take & (2 * CHIPS - 1), (8, 128))
     via = colour_nd * 4 + rank
-    via = jnp.sum(jnp.where(lane32 == own, via, 0), axis=1, keepdims=True)
-    out_ref[IDX3 : IDX3 + NEW, :] = jnp.broadcast_to(via, (NEW, 128))
-
-
-def matrices(cap_row, trans_row, out_ref):
+    via = jnp.sum(jnp.where(lane32 == lane_of(own), via, 0), axis=1, keepdims=True)
+    out_ref[IDX3 : IDX3 + NEW, :] = jnp.broadcast_to(via & (CHIPS - 1), (NEW, 128))
+
+
+def matrices(cap_in, trans_in, out_ref):
     shape = (SH, 128)
     k_of, lane = iota(shape, 0), iota(shape, 1)
     eye = k_of == lane
 
     def column(row):
-        return jnp.broadcast_to(jnp.sum(jnp.where(eye, row, 0.0), axis=1, keepdims=True), shape)
-
-    cap, tr = column(cap_row), column(trans_row)
+        square = iota((SH, SH), 0) == iota((SH, SH), 1)
+        return jnp.broadcast_to(jnp.sum(jnp.where(square, row, 0.0), axis=1, keepdims=True), shape)
+
+    cap, tr = column(cap_in), column(trans_in)
+    cap_row = jnp.sum(jnp.where(eye, cap, 0.0), axis=0, keepdims=True)
     inner = jnp.where(k_of == SH - 1, 0.0, pltpu.roll(tr, SH - 1, 0))
-    t0 = jnp.broadcast_to(trans_row[:, 0:1], shape)
+    t0 = jnp.broadcast_to(tr[0:1, :], shape)
     b = cap + tr + inner
     c = -inner
     a = jnp.where(k_of == 0, 0.0, -tr)
@@ -152,32 +167,16 @@
     asq = jnp.dot(amat[:, :SH], amat, precision=HI, preferred_element_type=F32)
     acouple = jnp.dot(amat[:, :SH], couple, precision=HI, preferred_element_type=F32)
     out_ref[0] = asq
-    out_ref[1] = t0 * column(amat[0:1, :])
-    out_ref[2] = t0 * column(asq[0:1, :])
+    out_ref[1] = t0 * column(amat[0:1, :SH])
+    out_ref[2] = t0 * column(asq[0:1, :SH])
     out_ref[3] = acouple
     out_ref[4] = couple
     out_ref[5, 0:8, :] = t0[0:8] * (1.0 - jnp.broadcast_to(couple[0:1], (8, 128)))
     out_ref[5, 8:16, :] = t0[0:8] * jnp.broadcast_to(acouple[0:1], (8, 128))
 
 
-def prepare_kernel(own_of, tab_ref, cap_ref, trans_ref, tbl_ref, mat_ref):
-    matrices(cap_ref[...], trans_ref[...], mat_ref)
-    route(own_of(), tab_ref[...], tbl_ref)
-
-
-def prepare(own_of, table, cap, tr, **more):
-    tab = jnp.pad(table.reshape(SLABS, NEW).T, ((0, 0), (0, 128 - SLABS)), constant_values=-1)
-    pad = lambda x: jnp.pad(x, (0, 128 - SH)).reshape(1, 128)
-    return pl.pallas_call(
-        functools.partial(prepare_kernel, own_of),
-        out_shape=(jax.ShapeDtypeStruct((56, 128), I32), jax.ShapeDtypeStruct((6, SH, 128), F32)),
-        in_specs=[pl.BlockSpec(memory_space=pltpu.VMEM)] * 3,
-        out_specs=[pl.BlockSpec(memory_space=pltpu.VMEM)] * 2,
-        **more,
-    )(tab, pad(cap), pad(tr))
-
-
 WIDE = 8
+CHUNKS = 2
 DEFAULTS = (1.0, 1.0, 0.0, 0.0, 0.0, 0.0, 0.0)
 NF = len(DEFAULTS)
 HALO = 2 * WIDE
@@ -185,15 +184,31 @@
 
 def move_kernel(
     slabs, cols,
-    tbl, p_ref, storage_ref, trans_ref, source_ref, old_ref, cb_ref, mat_ref,
+    table_hbm, cap_hbm, trans_row_hbm, cb_hbm, p_hbm, storage_hbm, trans_hbm, source_hbm, old_hbm,
     p_out, new_out,
+    table_ref, cap_ref, trans_row_ref, cb_ref, old_ref, mat_ref, tbl_ref, tbl,
     field, rows_in, edge_l, edge_r, from_l, from_r, line1, line2, shells1, shells2,
     stage1, mid, stage2, got, pb_stage, pb_mid,
-    halo_send, halo_recv, send1, recv1, send_pb, recv_pb, send2, recv2,
+    load, load_old, load_tbl, halo_send, halo_recv, send1, recv1, send_pb, recv_pb, send2, recv2,
 ):
     own, col = lax.axis_index("slab"), lax.axis_index("col")
     chip = own // 2
     first_core, second_core = own % 2 == 0, own % 2 == 1
+    loads = [
+        pltpu.make_async_copy(src, dst, load.at[i])
+        for i, (src, dst) in enumerate((
+            (table_hbm, table_ref), (cap_hbm, cap_ref), (trans_row_hbm, trans_row_ref), (cb_hbm, cb_ref),
+            (p_hbm, field.at[0]), (storage_hbm, field.at[1]), (trans_hbm, field.at[2]), (source_hbm, field.at[3]),
+        ))
+    ]
+    old_load = pltpu.make_async_copy(old_hbm, old_ref, load_old)
+    for one in loads:
+        one.start()
+
+    @pl.when(first_core)
+    def _():
+        old_load.start()
+
     neighbours = []
     for dr, dc in ((-1, 0), (1, 0), (0, -1), (0, 1), (-1, -1), (1, -1), (-1, 1), (1, 1)):
         ok = None
@@ -238,24 +253,33 @@
             return 0
         lax.fori_loop(1, slabs, body, 0)
 
+    for one in loads:
+        one.wait()
+    matrices(cap_ref[...], trans_row_ref[...], mat_ref)
+    route(own, by_owner(table_ref[...]), tbl_ref)
+    tbl_copy = pltpu.make_async_copy(tbl_ref, tbl, load_tbl)
+    tbl_copy.start()
+
     weight1, weight2 = mat_ref[1], mat_ref[2]
 
     @pl.when(first_core)
     def _():
+        old_load.wait()
+
         def body(o, _):
-            x = old_ref[o]
-            shells1[pl.ds(o, 1), :] = jnp.sum(x * weight1, axis=0, keepdims=True)
-            shells2[pl.ds(o, 1), :] = jnp.sum(x * weight2, axis=0, keepdims=True)
+            first, second = [], []
+            for j in range(8):
+                x = old_ref[8 * o + j]
+                first.append(jnp.sum(x * weight1, axis=0, keepdims=True))
+                second.append(jnp.sum(x * weight2, axis=0, keepdims=True))
+            shells1[pl.ds(8 * o, 8), :] = jnp.concatenate(first, axis=0)
+            shells2[pl.ds(8 * o, 8), :] = jnp.concatenate(second, axis=0)
             return 0
-        lax.fori_loop(0, OLD, body, 0)
+        lax.fori_loop(0, OLD // 8, body, 0)
 
     row64 = iota((64, 64), 0)
     blocks = cb_ref[...]
     hot = [(blocks == 2 * row64 + h).astype(F32) for h in range(2)]
-    field[0] = p_ref[...]
-    field[1] = storage_ref[...]
-    field[2] = trans_ref[...]
-    field[3] = source_ref[...]
 
     @pl.when(first_core)
     def _():
@@ -311,6 +335,15 @@
             device_id={"slab": 2 * m + 1}, device_id_type=MESH,
         )
 
+    def rows_of(c):
+        return pl.ds(SH // CHUNKS * c, SH // CHUNKS)
+
+    def chunk_to_middle(c, m):
+        src, dst = stage1.at[pl.ds(2 * m, 2), rows_of(c)], mid[c].at[pl.ds(2 * chip, 2)]
+        to_middle(src, dst, send1.at[c], recv1.at[c], m).start()
+
+    tbl_copy.wait()
+
     @pl.when(first_core)
     def _():
         square = mat_ref[0][:, :SH]
@@ -320,7 +353,7 @@
             for h in range(2):
                 slot = tbl[8 * h + m // 4, m % 4]
                 stage1[2 * m + h] = jnp.dot(square, old_ref[slot], precision=HI, preferred_element_type=F32)
-            to_middle(stage1.at[pl.ds(2 * m, 2)], mid.at[pl.ds(2 * chip, 2)], send1, recv1, m).start()
+            chunk_to_middle(0, m)
             return 0
         lax.fori_loop(0, CHIPS, body, 0)
 
@@ -396,37 +429,48 @@
             return 0
         lax.fori_loop(0, CHIPS, body, 0)
 
+        for c in range(1, CHUNKS):
+            def later(k, _):
+                chunk_to_middle(c, (chip + k) % CHIPS)
+                return 0
+            lax.fori_loop(0, CHIPS, later, 0)
+
     def await_bytes(ref, sem):
         pltpu.make_async_copy(ref, ref, sem).wait()
 
     @pl.when(second_core)
     def _():
-        await_bytes(mid, recv1)
-        await_bytes(pb_mid, recv_pb)
-        acouple, couple = mat_ref[3], mat_ref[4]
-
-        def block(d):
-            i = tbl[IDX2, d]
-            s, h = i // 2, i % 2
-            first = pb_mid[s, pl.ds(h, 1), :]
-            second = pb_mid[s, pl.ds(2 + h, 1), :]
-            return mid[i] + acouple * first + couple * second
-
-        def body(k, _):
-            d = (own + k) % slabs
-            stage2[d] = block(d)
-            pltpu.make_async_remote_copy(
-                src_ref=stage2.at[d], dst_ref=got.at[chip], send_sem=send2, recv_sem=recv2,
-                device_id={"slab": d}, device_id_type=MESH,
-            ).start()
-            return 0
-        lax.fori_loop(1, slabs, body, 0)
-        got[chip] = block(own)
-        await_bytes(got.at[pl.ds(0, CHIPS - 1)], recv2)
-
-    @pl.when(first_core)
-    def _():
-        await_bytes(got, recv2)
+        for c in range(CHUNKS):
+            rows = rows_of(c)
+            await_bytes(mid[c], recv1.at[c])
+            if c == 0:
+                await_bytes(pb_mid, recv_pb)
+            acouple, couple = mat_ref[3, rows], mat_ref[4, rows]
+
+            def block(d):
+                i = tbl[IDX2, lane_of(d)]
+                s, h = i // 2, i % 2
+                first = pb_mid[s, pl.ds(h, 1), :]
+                second = pb_mid[s, pl.ds(2 + h, 1), :]
+                return mid[c][i] + acouple * first + couple * second
+
+            def body(k, _):
+                d = (own + k) % slabs
+                stage2[d, rows] = block(d)
+                pltpu.make_async_remote_copy(
+                    src_ref=stage2.at[d, rows], dst_ref=got.at[chip, rows], send_sem=send2.at[c], recv_sem=recv2.at[c],
+                    device_id={"slab": d}, device_id_type=MESH,
+                ).start()
+                return 0
+            lax.fori_loop(1, slabs, body, 0)
+            got[chip, rows] = block(own)
+        for c in range(CHUNKS):
+            await_bytes(got.at[pl.ds(0, CHIPS - 1), rows_of(c)], recv2.at[c])
+
+    @pl.when(first_core)
+    def _():
+        for c in range(CHUNKS):
+            await_bytes(got.at[:, rows_of(c)], recv2.at[c])
 
     def gather(n, _):
         new_out[n] = got[tbl[IDX3 + n, 0]]
@@ -440,19 +484,20 @@
 
     @pl.when(first_core)
     def _():
-        await_bytes(stage1, send1)
+        for c in range(CHUNKS):
+            await_bytes(stage1.at[:, rows_of(c)], send1.at[c])
         await_bytes(pb_stage, send_pb)
 
     @pl.when(second_core)
     def _():
-        await_bytes(stage2.at[pl.ds(0, 2 * CHIPS - 1)], send2)
+        for c in range(CHUNKS):
+            await_bytes(stage2.at[pl.ds(0, 2 * CHIPS - 1), rows_of(c)], send2.at[c])
 
 
 def solution(mesh):
     slabs, cols = mesh.shape["slab"], mesh.shape["col"]
 
     def shards(pressure, storage, trans, source, shells_old, cap, tr, new_source, cell_block):
-        table, mats = prepare(lambda: lax.axis_index("slab"), new_source[0], cap, tr)
         vmem = pl.BlockSpec(memory_space=pltpu.VMEM)
         p, new = pl.pallas_call(
             functools.partial(move_kernel, slabs, cols),
@@ -460,9 +505,17 @@
                 jax.ShapeDtypeStruct((64, 256), F32),
                 jax.ShapeDtypeStruct((NEW, SH, 128), F32),
             ),
-            in_specs=[pl.BlockSpec(memory_space=pltpu.SMEM)] + [vmem] * 7,
+            in_specs=[pl.BlockSpec(memory_space=pl.ANY)] * 9,
             out_specs=[vmem] * 2,
             scratch_shapes=[
+                pltpu.VMEM((16, 128), I32),
+                pltpu.VMEM((1, SH), F32),
+                pltpu.VMEM((1, SH), F32),
+                pltpu.VMEM((1, OLD), I32),
+                pltpu.VMEM((OLD, SH, 128), F32),
+                pltpu.VMEM((6, SH, 128), F32),
+                pltpu.VMEM((56, 128), I32),
+                pltpu.SMEM((56, 128), I32),
                 pltpu.VMEM((NF, 64, 256), F32),
                 pltpu.VMEM((NF, HALO, 256), F32),
                 pltpu.VMEM((64, 128), F32),
@@ -474,18 +527,30 @@
                 pltpu.VMEM((OLD, 128), F32),
                 pltpu.VMEM((OLD, 128), F32),
                 pltpu.VMEM((2 * CHIPS, SH, 128), F32),
-                pltpu.VMEM((2 * CHIPS, SH, 128), F32),
+                tuple(pltpu.VMEM((2 * CHIPS, SH // CHUNKS, 128), F32) for _ in range(CHUNKS)),
                 pltpu.VMEM((2 * CHIPS, SH, 128), F32),
                 pltpu.VMEM((CHIPS, SH, 128), F32),
                 pltpu.VMEM((CHIPS, 8, 128), F32),
                 pltpu.VMEM((CHIPS, 8, 128), F32),
                 pltpu.SemaphoreType.DMA((8,)),
+                pltpu.SemaphoreType.DMA,
+                pltpu.SemaphoreType.DMA,
                 pltpu.SemaphoreType.DMA((8,)),
-            ] + [pltpu.SemaphoreType.DMA] * 6,
+                pltpu.SemaphoreType.DMA((8,)),
+                pltpu.SemaphoreType.DMA((CHUNKS,)),
+                pltpu.SemaphoreType.DMA((CHUNKS,)),
+                pltpu.SemaphoreType.DMA,
+                pltpu.SemaphoreType.DMA,
+                pltpu.SemaphoreType.DMA((CHUNKS,)),
+                pltpu.SemaphoreType.DMA((CHUNKS,)),
+            ],
             compiler_params=pltpu.CompilerParams(
-                collective_id=0, has_side_effects=True, vmem_limit_bytes=40 << 20
+                collective_id=0, has_side_effects=True, vmem_limit_bytes=60 << 20
             ),
-        )(table, pressure, storage, trans, source, shells_old[0], cell_block, mats)
+        )(
+            new_source.reshape(16, 128), cap.reshape(1, SH), tr.reshape(1, SH), cell_block,
+            pressure, storage, trans, source, shells_old[0],
+        )
         return p, new[None]
 
     f = P("slab", "col")

time: 85.5 us -> 67.6 us (0.79)
  Pallas kernels: 71.6 us -> 63 us
  local copies, waits for them, and re-layouts: 11.4 us -> 3.78 us
  other arithmetic: 1.36 us -> 0 us
    unnamed x19 -> x2, local copies, waits for them, and re-layouts: 9.39 us -> 3.78 us
    pallas_call x1 -> x0, Pallas kernels: 4.62 us -> none  [prepare(): pl.pallas_call(functools.partial(prepare_kernel, own_of), out_shape=(jax....]
    pallas_call x1, Pallas kernels: 66.9 us -> 63 us  [shards(): pl.pallas_call(functools.partial(move_kernel, slabs, cols), out_shape=(ja...]
    unnamed x1 -> x0, other arithmetic: 1.36 us -> none
    reshape x1 -> x0, local copies, waits for them, and re-layouts: 1.24 us -> none  [prepare(): pad = lambda x: jnp.pad(x, (0, 128 - SH)).reshape(1, 128)]
where the time goes in v2:
time: 67.6 us; the launch traced here: 67.4 us
  Pallas kernels  63 us (93%)
  local copies, waits for them, and re-layouts  3.78 us (6%)
    pallas_call x1, Pallas kernels, shards(): pl.pallas_call(functools.partial(move_kernel, slabs, cols), out_shape=(ja...  63 us
    unnamed x2, local copies, waits for them, and re-layouts  3.78 us

profile of v2, /device:TPU:1, one launch (start us, length us, event | category | flops | bytes accessed | tf_op | source)
XLA Modules:
  0.0 67.4 jit_solution(13926140663190355154)
XLA Ops:
  0.6 63.0 %shard_map.104 = (f32[64,256]{1,0:T(8,128)}, f32[32,64,128]{2,1,0:T(8,128)}) custom-call(s32[16,128]{1,0:T(8,128)} %bitcast.7, f32[1,64]{1,0:T(1,128)} %bitcast.8, f32[1,64]{1,0:T(1,128)} %bitcast.9, s32[1,64]{1,0:T(1,128)} %cb_hbm.1, f32[64,256]{1,0:T(8,128)} %p_hbm.1, f32[64,256]{1,0:T(8,128)} %storage_hbm.1, f32[64,256]{1,0:T(8,128)} %trans_hbm.1, ...), custom_call_target="tpu_custom_call" | custom-call | tf_op jit(solution)/shard_map/pallas_call | solution.py:502
  63.6 1.5 %copy.13 = f32[64,256]{1,0:T(8,128)} copy(f32[64,256]{1,0:T(8,128)} %get-tuple-element.8) | data formatting | bytes 131072
  65.1 2.3 %copy.14 = f32[1,32,64,128]{3,2,1,0:T(8,128)} copy(f32[1,32,64,128]{3,2,1,0:T(8,128)} %bitcast.6) | data formatting | bytes 2097152

commit v3 on v2

--- a/solution.py
+++ b/solution.py
@@ -176,7 +176,8 @@
 
 
 WIDE = 8
-CHUNKS = 2
+PARTS = (40, 24)
+CHUNKS = len(PARTS)
 DEFAULTS = (1.0, 1.0, 0.0, 0.0, 0.0, 0.0, 0.0)
 NF = len(DEFAULTS)
 HALO = 2 * WIDE
@@ -336,7 +337,7 @@
         )
 
     def rows_of(c):
-        return pl.ds(SH // CHUNKS * c, SH // CHUNKS)
+        return pl.ds(sum(PARTS[:c]), PARTS[c])
 
     def chunk_to_middle(c, m):
         src, dst = stage1.at[pl.ds(2 * m, 2), rows_of(c)], mid[c].at[pl.ds(2 * chip, 2)]
@@ -527,7 +528,7 @@
                 pltpu.VMEM((OLD, 128), F32),
                 pltpu.VMEM((OLD, 128), F32),
                 pltpu.VMEM((2 * CHIPS, SH, 128), F32),
-                tuple(pltpu.VMEM((2 * CHIPS, SH // CHUNKS, 128), F32) for _ in range(CHUNKS)),
+                tuple(pltpu.VMEM((2 * CHIPS, part, 128), F32) for part in PARTS),
                 pltpu.VMEM((2 * CHIPS, SH, 128), F32),
                 pltpu.VMEM((CHIPS, SH, 128), F32),
                 pltpu.VMEM((CHIPS, 8, 128), F32),
@@ -545,11 +546,13 @@
                 pltpu.SemaphoreType.DMA((CHUNKS,)),
             ],
             compiler_params=pltpu.CompilerParams(
-                collective_id=0, has_side_effects=True, vmem_limit_bytes=60 << 20
+                collective_id=0, has_side_effects=True, vmem_limit_bytes=40 << 20
             ),
         )(
-            new_source.reshape(16, 128), cap.reshape(1, SH), tr.reshape(1, SH), cell_block,
-            pressure, storage, trans, source, shells_old[0],
+            *(pltpu.with_memory_space_constraint(x, pltpu.HBM) for x in (
+                new_source.reshape(16, 128), cap.reshape(1, SH), tr.reshape(1, SH), cell_block,
+                pressure, storage, trans, source, shells_old[0],
+            ))
         )
         return p, new[None]
 

time: 67.6 us -> 63.9 us (0.945)
  local copies, waits for them, and re-layouts: 3.78 us -> 1.6 us
  Pallas kernels: 63 us -> 61.4 us
    unnamed x2, local copies, waits for them, and re-layouts: 3.78 us -> 1.6 us
    pallas_call x1, Pallas kernels: 63 us -> 61.4 us  [shards(): pl.pallas_call(functools.partial(move_kernel, slabs, cols), out_shape=(ja...]
where the time goes in v3:
time: 63.9 us; the launch traced here: 63.6 us
  Pallas kernels  61.4 us (96%)
  local copies, waits for them, and re-layouts  1.6 us (3%)
  between operations  0.64 us (1%)
    pallas_call x1, Pallas kernels, shards(): pl.pallas_call(functools.partial(move_kernel, slabs, cols), out_shape=(ja...  61.4 us
    unnamed x2, local copies, waits for them, and re-layouts  1.6 us

profile of v3, /device:TPU:1, one launch (start us, length us, event | category | flops | bytes accessed | tf_op | source)
XLA Modules:
  0.0 63.6 jit_solution(940547413586468909)
XLA Ops:
  0.6 61.4 %shard_map.104 = (f32[64,256]{1,0:T(8,128)S(1)}, f32[32,64,128]{2,1,0:T(8,128)S(1)}) custom-call(s32[16,128]{1,0:T(8,128)} %bitcast.7, f32[1,64]{1,0:T(1,128)} %bitcast.8, f32[1,64]{1,0:T(1,128)} %bitcast.9, s32[1,64]{1,0:T(1,128)} %cb_hbm.1, f32[64,256]{1,0:T(8,128)} %p_hbm.1, f32[64,256]{1,0:T(8,128)} %storage_hbm.1, f32[64,256]{1,0:T(8,128)} %trans_hbm.1, ...), custom_call_target="tpu_custom_call" | custom-call | tf_op jit(solution)/shard_map/pallas_call | solution.py:503
  62.0 0.6 copy.13
  62.6 1.0 %copy.14 = f32[1,32,64,128]{3,2,1,0:T(8,128)} copy(f32[1,32,64,128]{3,2,1,0:T(8,128)S(1)} %bitcast.5) | data formatting | bytes 2097152

commit v4 on v3

--- a/solution.py
+++ b/solution.py
@@ -459,24 +459,27 @@
                 d = (own + k) % slabs
                 stage2[d, rows] = block(d)
                 pltpu.make_async_remote_copy(
-                    src_ref=stage2.at[d, rows], dst_ref=got.at[chip, rows], send_sem=send2.at[c], recv_sem=recv2.at[c],
+                    src_ref=stage2.at[d, rows], dst_ref=got[c].at[chip], send_sem=send2.at[c], recv_sem=recv2.at[c],
                     device_id={"slab": d}, device_id_type=MESH,
                 ).start()
                 return 0
             lax.fori_loop(1, slabs, body, 0)
-            got[chip, rows] = block(own)
-        for c in range(CHUNKS):
-            await_bytes(got.at[pl.ds(0, CHIPS - 1), rows_of(c)], recv2.at[c])
-
-    @pl.when(first_core)
-    def _():
-        for c in range(CHUNKS):
-            await_bytes(got.at[:, rows_of(c)], recv2.at[c])
-
-    def gather(n, _):
-        new_out[n] = got[tbl[IDX3 + n, 0]]
-        return 0
-    lax.fori_loop(0, NEW, gather, 0)
+            got[c][chip] = block(own)
+
+    for c in range(CHUNKS):
+        @pl.when(second_core)
+        def _():
+            await_bytes(got[c].at[pl.ds(0, CHIPS - 1)], recv2.at[c])
+
+        @pl.when(first_core)
+        def _():
+            await_bytes(got[c], recv2.at[c])
+
+        def gather(n, _):
+            for j in range(4):
+                new_out[4 * n + j, rows_of(c)] = got[c][tbl[IDX3 + 4 * n + j, 0]]
+            return 0
+        lax.fori_loop(0, NEW // 4, gather, 0)
 
     for i, (ok, dr, dc) in enumerate(neighbours):
         @pl.when(ok)
@@ -530,7 +533,7 @@
                 pltpu.VMEM((2 * CHIPS, SH, 128), F32),
                 tuple(pltpu.VMEM((2 * CHIPS, part, 128), F32) for part in PARTS),
                 pltpu.VMEM((2 * CHIPS, SH, 128), F32),
-                pltpu.VMEM((CHIPS, SH, 128), F32),
+                tuple(pltpu.VMEM((CHIPS, part, 128), F32) for part in PARTS),
                 pltpu.VMEM((CHIPS, 8, 128), F32),
                 pltpu.VMEM((CHIPS, 8, 128), F32),
                 pltpu.SemaphoreType.DMA((8,)),

time: 63.9 us -> 63.7 us (level)
  no operation moved by 1% of the time
where the time goes in v4:
time: 63.7 us; the launch traced here: 63.4 us
  Pallas kernels  61.2 us (96%)
  local copies, waits for them, and re-layouts  1.6 us (3%)
  between operations  0.64 us (1%)
    pallas_call x1, Pallas kernels, shards(): pl.pallas_call(functools.partial(move_kernel, slabs, cols), out_shape=(ja...  61.2 us
    unnamed x2, local copies, waits for them, and re-layouts  1.6 us

profile of v4, /device:TPU:1, one launch (start us, length us, event | category | flops | bytes accessed | tf_op | source)
XLA Modules:
  0.0 63.4 jit_solution(3057812553551304729)
XLA Ops:
  0.6 61.2 %shard_map.104 = (f32[64,256]{1,0:T(8,128)S(1)}, f32[32,64,128]{2,1,0:T(8,128)S(1)}) custom-call(s32[16,128]{1,0:T(8,128)} %bitcast.7, f32[1,64]{1,0:T(1,128)} %bitcast.8, f32[1,64]{1,0:T(1,128)} %bitcast.9, s32[1,64]{1,0:T(1,128)} %cb_hbm.1, f32[64,256]{1,0:T(8,128)} %p_hbm.1, f32[64,256]{1,0:T(8,128)} %storage_hbm.1, f32[64,256]{1,0:T(8,128)} %trans_hbm.1, ...), custom_call_target="tpu_custom_call" | custom-call | tf_op jit(solution)/shard_map/pallas_call | solution.py:506
  61.8 0.6 copy.13
  62.5 1.0 %copy.14 = f32[1,32,64,128]{3,2,1,0:T(8,128)} copy(f32[1,32,64,128]{3,2,1,0:T(8,128)S(1)} %bitcast.5) | data formatting | bytes 2097152

commit v5 on v4

--- a/solution.py
+++ b/solution.py
@@ -243,16 +243,18 @@
     @pl.when(first_core)
     def _():
         def body(k, _):
-            greet(2 * ((chip + k) % CHIPS) + 1, col)
+            for j in range(8):
+                greet(2 * ((chip + 8 * k + j) % CHIPS) + 1, col)
             return 0
-        lax.fori_loop(0, CHIPS, body, 0)
+        lax.fori_loop(0, CHIPS // 8, body, 0)
 
     @pl.when(second_core)
     def _():
         def body(k, _):
-            greet((own + k) % slabs, col)
+            for j in range(9):
+                greet((own + 9 * k + j + 1) % slabs, col)
             return 0
-        lax.fori_loop(1, slabs, body, 0)
+        lax.fori_loop(0, (slabs - 1) // 9, body, 0)
 
     for one in loads:
         one.wait()

time: 63.7 us -> 63.9 us (level)
  no operation moved by 1% of the time
where the time goes in v5:
time: 63.9 us; the launch traced here: 63.6 us
  Pallas kernels  61.3 us (96%)
  local copies, waits for them, and re-layouts  1.6 us (3%)
  between operations  0.64 us (1%)
    pallas_call x1, Pallas kernels, shards(): pl.pallas_call(functools.partial(move_kernel, slabs, cols), out_shape=(ja...  61.3 us
    unnamed x2, local copies, waits for them, and re-layouts  1.6 us

profile of v5, /device:TPU:1, one launch (start us, length us, event | category | flops | bytes accessed | tf_op | source)
XLA Modules:
  0.0 63.6 jit_solution(10862913646508568866)
XLA Ops:
  0.6 61.3 %shard_map.104 = (f32[64,256]{1,0:T(8,128)S(1)}, f32[32,64,128]{2,1,0:T(8,128)S(1)}) custom-call(s32[16,128]{1,0:T(8,128)} %bitcast.7, f32[1,64]{1,0:T(1,128)} %bitcast.8, f32[1,64]{1,0:T(1,128)} %bitcast.9, s32[1,64]{1,0:T(1,128)} %cb_hbm.1, f32[64,256]{1,0:T(8,128)} %p_hbm.1, f32[64,256]{1,0:T(8,128)} %storage_hbm.1, f32[64,256]{1,0:T(8,128)} %trans_hbm.1, ...), custom_call_target="tpu_custom_call" | custom-call | tf_op jit(solution)/shard_map/pallas_call | solution.py:508
  62.0 0.6 copy.13
  62.6 1.0 %copy.14 = f32[1,32,64,128]{3,2,1,0:T(8,128)} copy(f32[1,32,64,128]{3,2,1,0:T(8,128)S(1)} %bitcast.5) | data formatting | bytes 2097152
